TPU v7x, 32 devices: a whole 2x2x4 slice. The times are simulated.
32 devices in a mesh: grp: 2 (over y), seq: 4 (over z), chan: 4 (over x, core).
Axes of the slice: x: 2, y: 2, z: 4, core: 2. Of those that a mesh axis runs over, the one named last changes fastest.
Arguments:
- inputs: bfloat16 [4, 1024, 1536], P('grp', 'seq', 'chan'), parts along dimension 0, may hold values from -30 to 30, as said below
- cotangent: bfloat16 [4, 1024, 1536], P('grp', 'seq', 'chan'), parts along dimension 0, may hold values from -6 to 6
- dilated_weight: bfloat16 [3, 1536, 768], P(None, None, 'chan'), may hold values from -0.09375 to 0.09375
- w_point: bfloat16 [1536, 768], P(None, 'chan'), may hold values from -0.21875 to 0.21875
- norm_gain: float32 [1536], replicated, may hold values from 0.1 to 1.9
Outputs:
- input_grad: bfloat16 [4, 1024, 1536], P('grp', 'seq', 'chan'), parts along dimension 0
- point_grad: float32 [3072, 768], P(('grp', 'seq'), 'chan'), parts along dimension 0
There are 2 independent parts, one for each index of `grp`. A program takes and returns all parts, laid end to end along the dimension named above; an argument that names none is the same for every part. Nothing has to cross between parts.
Inputs may be any that keep to these rules, and one draw needn't show every extreme that they name: `inputs`: the block's input activations.
All inputs are finite; a program needn't handle non-finite values.
Results may differ from a plain program's by a relative error of at most 0.007.
Values may be sent and summed in bfloat16 or wider, within the bound.
A program may use at most 64 MiB of HBM per device.

v0:
```python
import math

import jax
import jax.numpy as jnp
from jax import lax
from jax.sharding import PartitionSpec as P

DILATION_STEP = 512


epsilon = 1e-05


def passed_along(block, axis, distance):
    devices = range(lax.axis_size(axis))
    route = [(i - distance, i) for i in devices if i - distance in devices]
    return lax.ppermute(block, axis, route)


def gelu_value(values):
    return 0.5 * values * (1.0 + lax.erf(values * (1.0 / math.sqrt(2.0))))


def gelu_slope(values):
    return 0.5 * (1.0 + lax.erf(values * (1.0 / math.sqrt(2.0)))) + values * jnp.exp(
        -0.5 * values * values
    ) * (1.0 / math.sqrt(2.0 * math.pi))


def activate(whole_input, norm_gain):
    signal = whole_input.astype(jnp.float32)
    row_scale = lax.rsqrt(jnp.mean(signal * signal, axis=-1, keepdims=True) + epsilon)
    return (gelu_value(signal * row_scale * norm_gain).astype(jnp.bfloat16), row_scale)


def forward_tap_rows(values, weights):
    return jnp.einsum("bpc,ch->bph", values, weights, preferred_element_type=jnp.float32)


def backward_tap(values, weights):
    return jnp.einsum("bph,ch->bpc", values, weights, preferred_element_type=jnp.float32)


def per_device(inputs, cotangent, dilated_weight, w_point, norm_gain):
    stride_dev = DILATION_STEP // inputs.shape[1]
    whole_input, whole_grad = (
        lax.all_gather(inputs, "chan", axis=2, tiled=True),
        lax.all_gather(cotangent, "chan", axis=2, tiled=True),
    )
    hidden_state, row_scale = activate(whole_input, norm_gain)
    behind = passed_along(hidden_state, "seq", stride_dev)
    onward = passed_along(hidden_state, "seq", -stride_dev)
    dilated_output = (
        forward_tap_rows(behind, dilated_weight[0])
        + forward_tap_rows(hidden_state, dilated_weight[1])
        + forward_tap_rows(onward, dilated_weight[2])
    )
    activated = gelu_value(dilated_output).astype(jnp.bfloat16)
    hidden_grad = forward_tap_rows(whole_grad, w_point)
    dilated_output_grad = (hidden_grad * gelu_slope(dilated_output)).astype(jnp.bfloat16)
    gradient_after = passed_along(dilated_output_grad, "seq", -stride_dev)
    gradient_before = passed_along(dilated_output_grad, "seq", stride_dev)
    partial_grad = (
        backward_tap(gradient_after, dilated_weight[0])
        + backward_tap(dilated_output_grad, dilated_weight[1])
        + backward_tap(gradient_before, dilated_weight[2])
    )
    chan_width = inputs.shape[2]
    chan_index = lax.axis_index("chan")
    channels = norm_gain.shape[0]
    normed_grad = lax.psum_scatter(
        partial_grad.astype(jnp.bfloat16), "chan", scatter_dimension=2, tiled=True
    ).astype(jnp.float32)
    local_gain = lax.dynamic_slice_in_dim(norm_gain, chan_index * chan_width, chan_width)
    signal = inputs.astype(jnp.float32)
    unit = signal * row_scale
    scaled_grad = normed_grad * gelu_slope(unit * local_gain) * local_gain
    norm_total = lax.psum(jnp.sum(scaled_grad * unit, axis=-1, keepdims=True), "chan")
    branch_grad = row_scale * (scaled_grad - unit * (norm_total / channels))
    input_grad = (cotangent.astype(jnp.float32) + branch_grad).astype(jnp.bfloat16)
    flat_grad = whole_grad.reshape(-1, channels)
    flat_active = activated.reshape(-1, activated.shape[2])
    point_grad = lax.psum_scatter(
        lax.dot_general(
            flat_grad, flat_active, (((0,), (0,)), ((), ())), preferred_element_type=jnp.float32
        ),
        "seq",
        scatter_dimension=0,
        tiled=True,
    )
    return (input_grad, point_grad)


def solution(mesh):
    placed = (
        P("grp", "seq", "chan"),
        P("grp", "seq", "chan"),
        P(None, None, "chan"),
        P(None, "chan"),
        P(),
    )
    return jax.shard_map(
        per_device,
        mesh=mesh,
        in_specs=placed,
        out_specs=(P("grp", "seq", "chan"), P(("grp", "seq"), "chan")),
        check_vma=False,
    )
```

profile of v0, /device:TPU:0, one launch (start us, length us, event | category | flops | bytes accessed | tf_op | source)
XLA Modules:
  0.0 198.8 jit_solution(12688099044699035690)
XLA Ops:
  7.2 0.7 all-gather.3.cloned.1.call-update
  8.0 0.7 all-gather.5.cloned.1.call-update
  8.7 23.2 %all-gather.3.cloned.1.call-done = bf16[2,256,1536]{2,1,0:T(8,128)(2,1)} async-done(((bf16[2,256,384]{2,1,0:T(8,128)(2,1)}), bf16[2,256,1536]{2,1,0:T(8,128)(2,1)}) %all-gather.3.cloned.1.call-update) | async-done | bytes 1572880 | tf_op jit(solution)/shard_map/all_gather | solution.py:47
  32.0 1.9 fusion.1
  33.9 1.0 fusion.6
  35.0 1.3 collective-permute-start.1
  36.3 5.6 %collective-permute-start = (bf16[2,256,1536]{2,1,0:T(8,128)(2,1)S(1)}, bf16[2,256,1536]{2,1,0:T(8,128)(2,1)S(1)}, u32[]{:S(2)}, u32[]{:S(2)}) collective-permute-start(bf16[2,256,1536]{2,1,0:T(8,128)(2,1)S(1)} %fusion.6), channel_id=1, source_target_pairs={{0,8},{4,12},{1,9},{5,13},{2,10},{6,14},{3,11},{7,15},{16,24},{20,... | collective-permute-start | bytes 4718600 | tf_op jit(solution)/shard_map/ppermute | solution.py:17
  42.6 65.4 %collective-permute-done.1 = bf16[2,256,1536]{2,1,0:T(8,128)(2,1)S(1)} collective-permute-done((bf16[2,256,1536]{2,1,0:T(8,128)(2,1)S(1)}, bf16[2,256,1536]{2,1,0:T(8,128)(2,1)S(1)}, u32[]{:S(2)}, u32[]{:S(2)}) %collective-permute-start.1) | collective-permute-done | bytes 1572896 | tf_op jit(solution)/shard_map/ppermute | solution.py:17
  109.4 2.1 %fusion.40 = bf16[2,256,192]{1,2,0:T(8,128)(2,1)S(1)} fusion(f32[2,256,192]{1,2,0:T(8,128)S(1)} %fusion.10, bf16[2,256,1536]{2,1,0:T(8,128)(2,1)} %all-gather.5.cloned.1.call-done, bf16[1536,192]{0,1:T(8,128)(2,1)S(1)} %copy-done), kind=kOutput, calls=%fused_computation.50 | convolution fusion | flops 302972928 | bytes 2752512 | tf_op jit(solution)/shard_map/bpc,ch->bph/dot_general | solution.py:37
  111.5 1.5 collective-permute-start.3
  113.0 1.3 collective-permute-start.2
  114.9 1.9 collective-permute-done.3
  117.4 4.4 %collective-permute-done.2 = bf16[2,256,192]{1,2,0:T(8,128)(2,1)S(1)} collective-permute-done((bf16[2,256,192]{1,2,0:T(8,128)(2,1)S(1)}, bf16[2,256,192]{1,2,0:T(8,128)(2,1)S(1)}, u32[]{:S(2)}, u32[]{:S(2)}) %collective-permute-start.2) | collective-permute-done | bytes 196640 | tf_op jit(solution)/shard_map/ppermute | solution.py:17
  121.8 1.8 fusion.9
  123.6 3.7 %copy.7 = bf16[2,256,1536]{1,0,2:T(2,128)(2,1)S(1)} copy(bf16[2,256,1536]{2,1,0:T(8,128)(2,1)} %fusion.9) | data formatting | bytes 3145728
  127.2 1.5 copy.9
  128.8 1.3 copy-done.4
  130.1 1.5 convolution_bitcast_fusion
  131.8 28.4 %reduce-scatter.7.cloned.1.call-done = bf16[384,512]{1,0:T(8,128)(2,1)} async-done(((bf16[1536,512]{1,0:T(8,128)(2,1)}), bf16[384,512]{1,0:T(8,128)(2,1)}) %reduce-scatter.7.cloned.1.call-update) | async-done | bytes 393232
  160.2 1.1 reshape.22
  161.3 0.7 copy.8
  162.6 5.8 %psum.7 = f32[2,256,1]{1,0,2:T(2,128)S(1)} all-reduce(f32[2,256,1]{1,0,2:T(2,128)S(1)} %bitcast.45), channel_id=1, replica_groups=mesh['grp'=2,'seq'=4,'chan'=4] {'chan'}, use_global_device_ids=true, to_apply=%region_3.0 | all-reduce | flops 512 | bytes 4096 | tf_op jit(solution)/shard_map/psum | solution.py:78
  168.4 1.0 add_convert_fusion
  169.4 22.8 %reduce-scatter.5.cloned.1.call-done = f32[384,192]{0,1:T(8,128)} async-done(((f32[1536,192]{0,1:T(8,128)}), f32[384,192]{0,1:T(8,128)}) %reduce-scatter.5.cloned.1.call-update) | async-done | bytes 294928 | tf_op jit(solution)/shard_map/reduce_scatter | solution.py:83
  (30 shorter events, 4.2 us)
Async XLA Ops:
  7.2 102.2 %copy-start = (bf16[1536,192]{0,1:T(8,128)(2,1)S(1)}, bf16[1536,192]{0,1:T(8,128)(2,1)}, u32[]{:S(2)}) copy-start(bf16[1536,192]{0,1:T(8,128)(2,1)} %param.8) | copy-start | bytes 1769476
  7.2 26.7 %copy-start.6 = (f32[1536]{0:T(1024)S(1)}, f32[1536]{0:T(1024)}, u32[]{:S(2)}) copy-start(f32[1536]{0:T(1024)} %param.9) | copy-start | bytes 18436
  7.2 24.8 %all-gather.3.cloned.1.call-start = ((), (), s32[]{:S(2)}) async-start(), calls=%async_computation.2 | async-start | bytes 1966080 | tf_op jit(solution)/shard_map/all_gather | solution.py:47
  7.9 101.4 %all-gather.5.cloned.1.call-start = ((), (), s32[]{:S(2)}) async-start(), calls=%async_computation.3 | async-start | bytes 1966080 | tf_op jit(solution)/shard_map/all_gather | solution.py:48
  8.7 151.5 %reduce-scatter.7.cloned.1.call-start = ((), (), s32[]{:S(2)}) async-start(), calls=%async_computation.5 | async-start | bytes 1966080
  32.0 1.9 copy-start.1
  33.9 8.0 %copy-start.3 = (bf16[3,1536,192]{1,2,0:T(8,128)(2,1)S(1)}, bf16[3,1536,192]{1,2,0:T(8,128)(2,1)}, u32[]{:S(2)}) copy-start(bf16[3,1536,192]{1,2,0:T(8,128)(2,1)} %param.7) | copy-start | bytes 5308420
  35.0 73.0 %collective-permute-start.1 = (bf16[2,256,1536]{2,1,0:T(8,128)(2,1)S(1)}, bf16[2,256,1536]{2,1,0:T(8,128)(2,1)S(1)}, u32[]{:S(2)}, u32[]{:S(2)}) collective-permute-start(bf16[2,256,1536]{2,1,0:T(8,128)(2,1)S(1)} %fusion.6), channel_id=1, source_target_pairs={{8,0},{12,4},{9,1},{13,5},{10,2},{14,6},{11,3},{15,7},{24,16},{28,... | collective-permute-start | bytes 4718600 | tf_op jit(solution)/shard_map/ppermute | solution.py:17
  36.3 72.4 %collective-permute-start = (bf16[2,256,1536]{2,1,0:T(8,128)(2,1)S(1)}, bf16[2,256,1536]{2,1,0:T(8,128)(2,1)S(1)}, u32[]{:S(2)}, u32[]{:S(2)}) collective-permute-start(bf16[2,256,1536]{2,1,0:T(8,128)(2,1)S(1)} %fusion.6), channel_id=1, source_target_pairs={{0,8},{4,12},{1,9},{5,13},{2,10},{6,14},{3,11},{7,15},{16,24},{20,... | collective-permute-start | bytes 4718600 | tf_op jit(solution)/shard_map/ppermute | solution.py:17
  111.5 5.3 %collective-permute-start.3 = (bf16[2,256,192]{1,2,0:T(8,128)(2,1)S(1)}, bf16[2,256,192]{1,2,0:T(8,128)(2,1)S(1)}, u32[]{:S(2)}, u32[]{:S(2)}) collective-permute-start(bf16[2,256,192]{1,2,0:T(8,128)(2,1)S(1)} %fusion.40), channel_id=1, source_target_pairs={{0,8},{4,12},{1,9},{5,13},{2,10},{6,14},{3,11},{7,15},{16,24},{20,... | collective-permute-start | bytes 589832 | tf_op jit(solution)/shard_map/ppermute | solution.py:17
  113.0 8.8 %collective-permute-start.2 = (bf16[2,256,192]{1,2,0:T(8,128)(2,1)S(1)}, bf16[2,256,192]{1,2,0:T(8,128)(2,1)S(1)}, u32[]{:S(2)}, u32[]{:S(2)}) collective-permute-start(bf16[2,256,192]{1,2,0:T(8,128)(2,1)S(1)} %fusion.40), channel_id=1, source_target_pairs={{8,0},{12,4},{9,1},{13,5},{10,2},{14,6},{11,3},{15,7},{24,16},{28,... | collective-permute-start | bytes 589832 | tf_op jit(solution)/shard_map/ppermute | solution.py:17
  128.7 1.4 copy-start.4
  128.7 63.5 %reduce-scatter.5.cloned.1.call-start = ((), (), s32[]{:S(2)}) async-start(), calls=%async_computation.4 | async-start | bytes 1474560 | tf_op jit(solution)/shard_map/reduce_scatter | solution.py:83
  131.6 30.3 %copy-start.2 = (bf16[2,256,384]{2,1,0:T(8,128)(2,1)S(1)}, bf16[2,256,384]{2,1,0:T(8,128)(2,1)}, u32[]{:S(2)}) copy-start(bf16[2,256,384]{2,1,0:T(8,128)(2,1)} %param.5) | copy-start | bytes 1179652
  131.7 36.7 %copy-start.5 = (bf16[2,256,384]{2,1,0:T(8,128)(2,1)S(1)}, bf16[2,256,384]{2,1,0:T(8,128)(2,1)}, u32[]{:S(2)}) copy-start(bf16[2,256,384]{2,1,0:T(8,128)(2,1)} %param.6) | copy-start | bytes 1179652
Sparse Core Ops, SparseCore 0:
  9.6 22.3 all-gather.2
  33.5 19.6 all-gather.4
  128.9 31.2 reduce-scatter.6
  163.0 29.1 reduce-scatter.4
where the time goes:
time: 199 us
  waiting for transfers between devices  148 us (74%)
  between operations  14 us (7%)
  starting transfers between devices  9.85 us (5%)
  matrix products  8.55 us (4%)
  local copies, waits for them, and re-layouts  8.36 us (4%)
  blocking collectives  5.76 us (3%)
  other arithmetic  4.65 us (2%)
    ppermute x4, waiting for transfers between devices, passed_along(): return lax.ppermute(block, axis, route)  71.8 us
    unnamed x5, waiting for transfers between devices  29.8 us
    all_gather x1, waiting for transfers between devices, per_device(): lax.all_gather(inputs, 'chan', axis=2, tiled=True)  23.2 us
    reduce_scatter x1, waiting for transfers between devices, per_device(): lax.psum_scatter(lax.dot_general(flat_grad, flat_active, (((0,), (0,)), (...  22.8 us
    ppermute x4, starting transfers between devices, passed_along(): return lax.ppermute(block, axis, route)  9.69 us
    unnamed x18, local copies, waits for them, and re-layouts  8.28 us
    psum x1, blocking collectives, per_device(): lax.psum(jnp.sum(scaled_grad * unit, axis=-1, keepdims=True), 'chan')  5.76 us
    dot_general x4, matrix products, forward_tap_rows(): jnp.einsum('bpc,ch->bph', values, weights, preferred_element_type=jnp.flo...  4.08 us
  transfers between devices with their start and end apart: 8, of which 6 were waited for; matrix products, arithmetic and copies ran while one was open for 6% of the time, Pallas kernels for 0%

commit v1 on v0

--- a/solution.py
+++ b/solution.py
@@ -48,12 +48,16 @@
         lax.all_gather(cotangent, "chan", axis=2, tiled=True),
     )
     hidden_state, row_scale = activate(whole_input, norm_gain)
-    behind = passed_along(hidden_state, "seq", stride_dev)
-    onward = passed_along(hidden_state, "seq", -stride_dev)
+    behind = passed_along(
+        forward_tap_rows(hidden_state, dilated_weight[0]).astype(jnp.bfloat16), "seq", stride_dev
+    )
+    onward = passed_along(
+        forward_tap_rows(hidden_state, dilated_weight[2]).astype(jnp.bfloat16), "seq", -stride_dev
+    )
     dilated_output = (
-        forward_tap_rows(behind, dilated_weight[0])
+        behind.astype(jnp.float32)
         + forward_tap_rows(hidden_state, dilated_weight[1])
-        + forward_tap_rows(onward, dilated_weight[2])
+        + onward.astype(jnp.float32)
     )
     activated = gelu_value(dilated_output).astype(jnp.bfloat16)
     hidden_grad = forward_tap_rows(whole_grad, w_point)

time: 199 us -> 145 us (0.73)
  waiting for transfers between devices: 148 us -> 93 us
    ppermute x4, waiting for transfers between devices: 71.8 us -> 12.9 us  [passed_along(): return lax.ppermute(block, axis, route)]
    all_gather x1, waiting for transfers between devices: 0.02 us -> 10.2 us  [per_device(): lax.all_gather(cotangent, 'chan', axis=2, tiled=True)]
    unnamed x5, waiting for transfers between devices: 29.8 us -> 24 us
  transfers between devices with their start and end apart: 8 -> 8, of which waited for: 6 -> 7; matrix products, arithmetic and copies ran while one was open for 6% -> 8% of each run, Pallas kernels for 0% -> 0%
where the time goes in v1:
time: 145 us
  waiting for transfers between devices  93 us (64%)
  between operations  13.9 us (10%)
  starting transfers between devices  9.8 us (7%)
  local copies, waits for them, and re-layouts  8.74 us (6%)
  matrix products  8.62 us (6%)
  blocking collectives  5.76 us (4%)
  other arithmetic  4.65 us (3%)
    unnamed x5, waiting for transfers between devices  24 us
    all_gather x1, waiting for transfers between devices, per_device(): lax.all_gather(inputs, 'chan', axis=2, tiled=True)  23.2 us
    reduce_scatter x1, waiting for transfers between devices, per_device(): lax.psum_scatter(lax.dot_general(flat_grad, flat_active, (((0,), (0,)), (...  22.8 us
    ppermute x4, waiting for transfers between devices, passed_along(): return lax.ppermute(block, axis, route)  12.9 us
    all_gather x1, waiting for transfers between devices, per_device(): lax.all_gather(cotangent, 'chan', axis=2, tiled=True)  10.2 us
    ppermute x4, starting transfers between devices, passed_along(): return lax.ppermute(block, axis, route)  9.65 us
    unnamed x18, local copies, waits for them, and re-layouts  8.66 us
    psum x1, blocking collectives, per_device(): lax.psum(jnp.sum(scaled_grad * unit, axis=-1, keepdims=True), 'chan')  5.76 us
  transfers between devices with their start and end apart: 8, of which 7 were waited for; matrix products, arithmetic and copies ran while one was open for 8% of the time, Pallas kernels for 0%

profile of v1, /device:TPU:0, one launch (start us, length us, event | category | flops | bytes accessed | tf_op | source)
XLA Modules:
  0.0 144.5 jit_solution(14405038946688367483)
XLA Ops:
  7.2 0.7 all-gather.3.cloned.1.call-update
  8.0 0.7 all-gather.5.cloned.1.call-update
  8.7 23.2 %all-gather.3.cloned.1.call-done = bf16[2,256,1536]{2,1,0:T(8,128)(2,1)} async-done(((bf16[2,256,384]{2,1,0:T(8,128)(2,1)}), bf16[2,256,1536]{2,1,0:T(8,128)(2,1)}) %all-gather.3.cloned.1.call-update) | async-done | bytes 1572880 | tf_op jit(solution)/shard_map/all_gather | solution.py:47
  32.0 1.9 %fusion.1 = f32[2,256]{1,0:T(2,128)S(1)} fusion(bf16[2,256,1536]{2,1,0:T(8,128)(2,1)} %all-gather.3.cloned.1.call-done), kind=kLoop, calls=%fused_computation.4 | loop fusion | flops 2358784 | bytes 1574912 | tf_op jit(solution)/shard_map/reduce_sum | solution.py:32
  33.9 1.0 fusion.6
  36.0 4.3 %collective-permute-start = (bf16[2,256,192]{1,2,0:T(8,128)(2,1)S(1)}, bf16[2,256,192]{1,2,0:T(8,128)(2,1)S(1)}, u32[]{:S(2)}, u32[]{:S(2)}) collective-permute-start(bf16[2,256,192]{1,2,0:T(8,128)(2,1)S(1)} %convolution_convert_fusion.1), channel_id=1, source_target_pairs={{0,8},{4,12},{1,9},{5,13},{2,10},{6,14},{3,11},{7,15},{16,24},{20,... | collective-permute-start | bytes 589832 | tf_op jit(solution)/shard_map/ppermute | solution.py:17
  41.0 1.3 collective-permute-start.1
  43.0 10.2 %all-gather.5.cloned.1.call-done = bf16[2,256,1536]{2,1,0:T(8,128)(2,1)} async-done(((bf16[2,256,384]{2,1,0:T(8,128)(2,1)}), bf16[2,256,1536]{2,1,0:T(8,128)(2,1)}) %all-gather.5.cloned.1.call-update) | async-done | bytes 1572880 | tf_op jit(solution)/shard_map/all_gather | solution.py:48
  53.2 1.6 %collective-permute-done.1 = bf16[2,256,192]{1,2,0:T(8,128)(2,1)S(1)} collective-permute-done((bf16[2,256,192]{1,2,0:T(8,128)(2,1)S(1)}, bf16[2,256,192]{1,2,0:T(8,128)(2,1)S(1)}, u32[]{:S(2)}, u32[]{:S(2)}) %collective-permute-start.1) | collective-permute-done | bytes 196640 | tf_op jit(solution)/shard_map/ppermute | solution.py:17
  54.8 2.2 %fusion.38 = bf16[2,256,192]{1,2,0:T(8,128)(2,1)S(1)} fusion(bf16[2,256,192]{1,2,0:T(8,128)(2,1)S(1)} %collective-permute-done.1, f32[2,256,192]{1,2,0:T(8,128)S(1)} %fusion.21, bf16[2,256,192]{1,2,0:T(8,128)(2,1)S(1)} %collective-permute-done, bf16[2,256,1536]{2,1,0:T(8,128)(2,1)} %all-gather.5.cloned.1.call-done, bf16[1536,192]{0,1:T(8,128)(2,1)S(1)} %copy-done), kind=kOutput, calls=%fused_computation.49 | convolution fusion | flops 303366144 | bytes 3145728 | tf_op jit(solution)/shard_map/bpc,ch->bph/dot_general | solution.py:37
  56.9 2.7 %collective-permute-start.3 = (bf16[2,256,192]{1,2,0:T(8,128)(2,1)S(1)}, bf16[2,256,192]{1,2,0:T(8,128)(2,1)S(1)}, u32[]{:S(2)}, u32[]{:S(2)}) collective-permute-start(bf16[2,256,192]{1,2,0:T(8,128)(2,1)S(1)} %fusion.38), channel_id=1, source_target_pairs={{0,8},{4,12},{1,9},{5,13},{2,10},{6,14},{3,11},{7,15},{16,24},{20,... | collective-permute-start | bytes 589832 | tf_op jit(solution)/shard_map/ppermute | solution.py:17
  59.7 1.3 collective-permute-start.2
  61.6 2.7 %collective-permute-done.3 = bf16[2,256,192]{1,2,0:T(8,128)(2,1)S(1)} collective-permute-done((bf16[2,256,192]{1,2,0:T(8,128)(2,1)S(1)}, bf16[2,256,192]{1,2,0:T(8,128)(2,1)S(1)}, u32[]{:S(2)}, u32[]{:S(2)}) %collective-permute-start.3) | collective-permute-done | bytes 196640 | tf_op jit(solution)/shard_map/ppermute | solution.py:17
  64.9 8.6 %collective-permute-done.2 = bf16[2,256,192]{1,2,0:T(8,128)(2,1)S(1)} collective-permute-done((bf16[2,256,192]{1,2,0:T(8,128)(2,1)S(1)}, bf16[2,256,192]{1,2,0:T(8,128)(2,1)S(1)}, u32[]{:S(2)}, u32[]{:S(2)}) %collective-permute-start.2) | collective-permute-done | bytes 196640 | tf_op jit(solution)/shard_map/ppermute | solution.py:17
  73.5 1.8 %fusion.9 = bf16[2,256,1536]{2,1,0:T(8,128)(2,1)} fusion(f32[2,256,1536]{2,1,0:T(8,128)S(1)} %fusion.16, f32[2,256,1536]{2,1,0:T(8,128)S(1)} %fusion.19, bf16[2,256,192]{1,2,0:T(8,128)(2,1)S(1)} %collective-permute-done.2, bf16[3,1536,192]{1,2,0:T(8,128)(2,1)S(1)} %copy-done.3), kind=kOutput, calls=%fused_computation.12 | convolution fusion | flops 304349184 | bytes 8650752 | tf_op jit(solution)/shard_map/bph,ch->bpc/dot_general | solution.py:41
  75.2 3.7 %copy.7 = bf16[2,256,1536]{1,0,2:T(2,128)(2,1)S(1)} copy(bf16[2,256,1536]{2,1,0:T(8,128)(2,1)} %fusion.9) | data formatting | bytes 3145728
  78.9 1.5 %copy.9 = bf16[192,8,2,256]{3,1,2,0:T(8,128)(2,1)} copy(bf16[192,8,2,256]{3,2,1,0:T(2,128)(2,1)S(1)} %bitcast.43) | data formatting | bytes 3145728
  80.5 1.3 copy-done.4
  81.8 1.5 %convolution_bitcast_fusion = f32[1536,192]{0,1:T(8,128)} fusion(bf16[2,256,1536]{2,1,0:T(8,128)(2,1)S(1)} %copy-done.4, bf16[2,256,192]{1,2,0:T(8,128)(2,1)S(1)} %collective-permute-done.1, f32[2,256,192]{1,2,0:T(8,128)S(1)} %fusion.21, bf16[2,256,192]{1,2,0:T(8,128)(2,1)S(1)} %collective-permute-done), kind=kOutput, calls=%fused_computation.13 | convolution fusion | flops 302874624 | bytes 3538944 | tf_op jit(solution)/shard_map/dot_general | solution.py:88
  83.4 22.5 %reduce-scatter.7.cloned.1.call-done = bf16[384,512]{1,0:T(8,128)(2,1)} async-done(((bf16[1536,512]{1,0:T(8,128)(2,1)}), bf16[384,512]{1,0:T(8,128)(2,1)}) %reduce-scatter.7.cloned.1.call-update) | async-done | bytes 393232
  106.0 1.1 reshape.22
  108.4 5.8 %psum.7 = f32[2,256,1]{1,0,2:T(2,128)S(1)} all-reduce(f32[2,256,1]{1,0,2:T(2,128)S(1)} %bitcast.45), channel_id=1, replica_groups=mesh['grp'=2,'seq'=4,'chan'=4] {'chan'}, use_global_device_ids=true, to_apply=%region_3.0 | all-reduce | flops 512 | bytes 4096 | tf_op jit(solution)/shard_map/psum | solution.py:82
  114.2 1.0 add_convert_fusion
  115.2 22.8 %reduce-scatter.5.cloned.1.call-done = f32[384,192]{0,1:T(8,128)} async-done(((f32[1536,192]{0,1:T(8,128)}), f32[384,192]{0,1:T(8,128)}) %reduce-scatter.5.cloned.1.call-update) | async-done | bytes 294928 | tf_op jit(solution)/shard_map/reduce_scatter | solution.py:87
  (30 shorter events, 5.2 us)
Async XLA Ops:
  7.2 47.6 %copy-start = (bf16[1536,192]{0,1:T(8,128)(2,1)S(1)}, bf16[1536,192]{0,1:T(8,128)(2,1)}, u32[]{:S(2)}) copy-start(bf16[1536,192]{0,1:T(8,128)(2,1)} %param.8) | copy-start | bytes 1769476
  7.2 26.7 %copy-start.6 = (f32[1536]{0:T(1024)S(1)}, f32[1536]{0:T(1024)}, u32[]{:S(2)}) copy-start(f32[1536]{0:T(1024)} %param.9) | copy-start | bytes 18436
  7.2 24.8 %all-gather.3.cloned.1.call-start = ((), (), s32[]{:S(2)}) async-start(), calls=%async_computation.2 | async-start | bytes 1966080 | tf_op jit(solution)/shard_map/all_gather | solution.py:47
  7.9 45.3 %all-gather.5.cloned.1.call-start = ((), (), s32[]{:S(2)}) async-start(), calls=%async_computation.3 | async-start | bytes 1966080 | tf_op jit(solution)/shard_map/all_gather | solution.py:48
  8.7 97.3 %reduce-scatter.7.cloned.1.call-start = ((), (), s32[]{:S(2)}) async-start(), calls=%async_computation.5 | async-start | bytes 1966080
  32.0 1.9 %copy-start.1 = (bf16[2,256,1536]{2,1,0:T(8,128)(2,1)S(1)}, bf16[2,256,1536]{2,1,0:T(8,128)(2,1)}, u32[]{:S(2)}) copy-start(bf16[2,256,1536]{2,1,0:T(8,128)(2,1)} %all-gather.3.cloned.1.call-done) | copy-start | bytes 4718596
  33.9 1.5 %copy-start.3 = (bf16[3,1536,192]{1,2,0:T(8,128)(2,1)S(1)}, bf16[3,1536,192]{1,2,0:T(8,128)(2,1)}, u32[]{:S(2)}) copy-start(bf16[3,1536,192]{1,2,0:T(8,128)(2,1)} %param.7) | copy-start | bytes 5308420
  36.0 17.2 %collective-permute-start = (bf16[2,256,192]{1,2,0:T(8,128)(2,1)S(1)}, bf16[2,256,192]{1,2,0:T(8,128)(2,1)S(1)}, u32[]{:S(2)}, u32[]{:S(2)}) collective-permute-start(bf16[2,256,192]{1,2,0:T(8,128)(2,1)S(1)} %convolution_convert_fusion.1), channel_id=1, source_target_pairs={{0,8},{4,12},{1,9},{5,13},{2,10},{6,14},{3,11},{7,15},{16,24},{20,... | collective-permute-start | bytes 589832 | tf_op jit(solution)/shard_map/ppermute | solution.py:17
  41.0 13.8 %collective-permute-start.1 = (bf16[2,256,192]{1,2,0:T(8,128)(2,1)S(1)}, bf16[2,256,192]{1,2,0:T(8,128)(2,1)S(1)}, u32[]{:S(2)}, u32[]{:S(2)}) collective-permute-start(bf16[2,256,192]{1,2,0:T(8,128)(2,1)S(1)} %convolution_convert_fusion), channel_id=1, source_target_pairs={{8,0},{12,4},{9,1},{13,5},{10,2},{14,6},{11,3},{15,7},{24,16},{28,... | collective-permute-start | bytes 589832 | tf_op jit(solution)/shard_map/ppermute | solution.py:17
  56.9 7.3 %collective-permute-start.3 = (bf16[2,256,192]{1,2,0:T(8,128)(2,1)S(1)}, bf16[2,256,192]{1,2,0:T(8,128)(2,1)S(1)}, u32[]{:S(2)}, u32[]{:S(2)}) collective-permute-start(bf16[2,256,192]{1,2,0:T(8,128)(2,1)S(1)} %fusion.38), channel_id=1, source_target_pairs={{0,8},{4,12},{1,9},{5,13},{2,10},{6,14},{3,11},{7,15},{16,24},{20,... | collective-permute-start | bytes 589832 | tf_op jit(solution)/shard_map/ppermute | solution.py:17
  59.7 13.8 %collective-permute-start.2 = (bf16[2,256,192]{1,2,0:T(8,128)(2,1)S(1)}, bf16[2,256,192]{1,2,0:T(8,128)(2,1)S(1)}, u32[]{:S(2)}, u32[]{:S(2)}) collective-permute-start(bf16[2,256,192]{1,2,0:T(8,128)(2,1)S(1)} %fusion.38), channel_id=1, source_target_pairs={{8,0},{12,4},{9,1},{13,5},{10,2},{14,6},{11,3},{15,7},{24,16},{28,... | collective-permute-start | bytes 589832 | tf_op jit(solution)/shard_map/ppermute | solution.py:17
  80.4 1.4 copy-start.4
  80.4 57.6 %reduce-scatter.5.cloned.1.call-start = ((), (), s32[]{:S(2)}) async-start(), calls=%async_computation.4 | async-start | bytes 1474560 | tf_op jit(solution)/shard_map/reduce_scatter | solution.py:87
  83.3 24.4 %copy-start.2 = (bf16[2,256,384]{2,1,0:T(8,128)(2,1)S(1)}, bf16[2,256,384]{2,1,0:T(8,128)(2,1)}, u32[]{:S(2)}) copy-start(bf16[2,256,384]{2,1,0:T(8,128)(2,1)} %param.5) | copy-start | bytes 1179652
  83.3 30.9 %copy-start.5 = (bf16[2,256,384]{2,1,0:T(8,128)(2,1)S(1)}, bf16[2,256,384]{2,1,0:T(8,128)(2,1)}, u32[]{:S(2)}) copy-start(bf16[2,256,384]{2,1,0:T(8,128)(2,1)} %param.6) | copy-start | bytes 1179652
Sparse Core Ops, SparseCore 0:
  9.6 22.3 all-gather.2
  33.5 19.6 all-gather.4
  80.5 25.3 reduce-scatter.6
  108.8 29.1 reduce-scatter.4

commit v2 on v0

v2 whole, which is shorter than its diff:
```python
import functools
import math

import jax
import jax.numpy as jnp
from jax import lax
from jax.experimental import pallas as pl
from jax.experimental.pallas import tpu as pltpu
from jax.sharding import PartitionSpec as P

DILATION_STEP = 512
epsilon = 1e-05
N_SEMS = 64
F32 = jnp.float32
BF16 = jnp.bfloat16
MESH = pl.DeviceIdType.MESH


def gelu_value(values):
    return 0.5 * values * (1.0 + lax.erf(values * (1.0 / math.sqrt(2.0))))


def gelu_slope(values):
    return 0.5 * (1.0 + lax.erf(values * (1.0 / math.sqrt(2.0)))) + values * jnp.exp(
        -0.5 * values * values
    ) * (1.0 / math.sqrt(2.0 * math.pi))


def dot_nn(a, b):
    return lax.dot_general(a, b, (((1,), (0,)), ((), ())), preferred_element_type=F32)


def dot_nt(a, b):
    return lax.dot_general(a, b, (((1,), (1,)), ((), ())), preferred_element_type=F32)


def dot_tn(a, b):
    return lax.dot_general(a, b, (((0,), (0,)), ((), ())), preferred_element_type=F32)


def lanes_to_row(values):
    total = values[:, 0:128]
    for at in range(128, values.shape[1], 128):
        total = total + values[:, at : at + 128]
    return jnp.sum(total.T, axis=0, keepdims=True)


def row_to_columns(row):
    return jnp.broadcast_to(row, (128, 128)).T


def widen(columns, width):
    return jnp.concatenate([columns] * (width // 128), axis=1)


def kernel(
    seq_n, stride, scatter, x_ref, ct_ref, w_ref, wp_ref, gain_ref, out_ref, pg_ref,
    hid, cot, ss, rs, slope, dil, acc_lo, acc_hi, act, hg, y_lo, y_hi, yr_lo, yr_hi, dg, dr_lo, dr_hi,
    part, ps, pr, xs, xr, sg, pn, qs, qr, qs2, qr2, send_sem, recv_sem,
):
    batch, rows, width = x_ref.shape
    channels = gain_ref.shape[1]
    c = lax.axis_index("chan")
    s = lax.axis_index("seq")
    c1 = c + 1 - 2 * lax.rem(c, 2)
    c2 = lax.rem(c + 2, 4)
    c3 = 3 - c
    peers = (c, c1, c2, c3)
    s1 = s + 1 - 2 * lax.rem(s, 2)
    s2 = lax.rem(s + 2, 4)
    s3 = 3 - s
    has_hi = s + stride < seq_n
    has_lo = s >= stride
    up = lax.rem(s + stride, seq_n)
    down = lax.rem(s - stride + seq_n, seq_n)

    count = [0]
    sent = []

    def copy(src, dst, device):
        k = count[0]
        count[0] += 1
        return pltpu.make_async_remote_copy(
            src_ref=src, dst_ref=dst, send_sem=send_sem.at[k], recv_sem=recv_sem.at[k],
            device_id=device, device_id_type=MESH,
        )

    def push(src, dst, device):
        handle = copy(src, dst, device)
        handle.start()
        sent.append(handle)
        return handle

    def chan_rows(ch):
        return pl.ds(pl.multiple_of(ch * width, width), width)

    barrier = pltpu.get_barrier_semaphore()
    for peer in (c1, c2, c3):
        pl.semaphore_signal(barrier, inc=1, device_id={"chan": peer}, device_id_type=MESH)

    @pl.when(has_hi)
    def _():
        pl.semaphore_signal(barrier, inc=1, device_id={"seq": up}, device_id_type=MESH)

    @pl.when(has_lo)
    def _():
        pl.semaphore_signal(barrier, inc=1, device_id={"seq": down}, device_id_type=MESH)

    if scatter:
        pl.semaphore_signal(barrier, inc=1, device_id={"seq": s1}, device_id_type=MESH)

    for b in range(batch):
        for at in range(0, rows, 128):
            v = x_ref[b, at : at + 128, :].astype(F32)
            ss[0, :, b * rows + at : b * rows + at + 128] = jnp.broadcast_to(lanes_to_row(v * v), (8, 128))

    cot[c] = ct_ref[...]
    ways = has_hi.astype(jnp.int32) + has_lo.astype(jnp.int32)
    pl.semaphore_wait(barrier, ways + (4 if scatter else 3))

    ss_in = [push(ss.at[0], ss.at[k], {"chan": peers[k]}) for k in (2, 3, 1)]
    cot_in = [[None] * batch for _ in range(4)]
    hid_in = [[None] * batch for _ in range(4)]

    def spread_cot(b):
        cot_in[2][b] = push(cot.at[c, b], cot.at[c, b], {"chan": c2})
        cot_in[1][b] = push(cot.at[c, b], cot.at[c, b], {"chan": c1})

    def relay_cot(b):
        copy_in = cot_in[2][b]
        copy_in.wait_recv()
        cot_in[3][b] = push(cot.at[c2, b], cot.at[c2, b], {"chan": c1})

    spread_cot(0)
    for handle in ss_in:
        handle.wait_recv()
    gain = gain_ref[:, chan_rows(c)]
    for b in range(batch):
        for at in range(0, rows, 128):
            here = slice(b * rows + at, b * rows + at + 128)
            total = ss[0, 0:1, here] + ss[1, 0:1, here] + ss[2, 0:1, here] + ss[3, 0:1, here]
            columns = row_to_columns(lax.rsqrt(total * (1.0 / channels) + epsilon))
            rs[b, at : at + 128, :] = columns
            normed = x_ref[b, at : at + 128, :].astype(F32) * widen(columns, width) * gain
            hid[0, b, at : at + 128, :] = gelu_value(normed).astype(BF16)
        hid_in[2][b] = push(hid.at[0, b], hid.at[2, b], {"chan": c2})
        hid_in[1][b] = push(hid.at[0, b], hid.at[1, b], {"chan": c1})
    for b in range(1, batch):
        spread_cot(b)

    def normed_slope(b):
        for at in range(0, rows, 128):
            normed = x_ref[b, at : at + 128, :].astype(F32) * widen(rs[b, at : at + 128, :], width) * gain
            slope[b, at : at + 128, :] = gelu_slope(normed) * gain

    normed_slope(0)
    relay_cot(0)

    halo = [None] * batch
    for b in range(batch):
        for k in range(4):
            if k > 0:
                hid_in[k][b].wait_recv()
            if k == 2:
                hid_in[3][b] = push(hid.at[2, b], hid.at[3, b], {"chan": c1})
            w_rows = chan_rows(peers[k])

            @pl.when(has_hi)
            def _():
                term = dot_nn(hid[k, b], w_ref[0, w_rows, :])
                acc_hi[...] = term if k == 0 else acc_hi[...] + term

            @pl.when(has_lo)
            def _():
                term = dot_nn(hid[k, b], w_ref[2, w_rows, :])
                acc_lo[...] = term if k == 0 else acc_lo[...] + term

        to_hi = copy(y_hi.at[b], yr_lo.at[b], {"seq": up})
        to_lo = copy(y_lo.at[b], yr_hi.at[b], {"seq": down})
        halo[b] = (to_hi, to_lo)

        @pl.when(has_hi)
        def _():
            y_hi[b] = acc_hi[...].astype(BF16)
            to_hi.start()

        @pl.when(has_lo)
        def _():
            y_lo[b] = acc_lo[...].astype(BF16)
            to_lo.start()

        dil[b] = sum(dot_nn(hid[k, b], w_ref[1, chan_rows(peers[k]), :]) for k in range(4))

    def hidden_grad(b):
        cot_in[1][b].wait_recv()
        cot_in[3][b].wait_recv()
        hg[b] = sum(dot_nn(cot[j, b], wp_ref[j * width : (j + 1) * width, :]) for j in range(4))

    hidden_grad(0)
    for b in range(1, batch):
        normed_slope(b)
        relay_cot(b)

    back = [None] * batch
    for b in range(batch):
        to_hi, to_lo = halo[b]

        @pl.when(has_lo)
        def _():
            to_hi.wait_recv()
            dil[b] += yr_lo[b].astype(F32)

        @pl.when(has_hi)
        def _():
            to_lo.wait_recv()
            dil[b] += yr_hi[b].astype(F32)

        if b > 0:
            hidden_grad(b)
        value = dil[b]
        dg[b] = (hg[b] * gelu_slope(value)).astype(BF16)
        g_hi = copy(dg.at[b], dr_lo.at[b], {"seq": up})
        g_lo = copy(dg.at[b], dr_hi.at[b], {"seq": down})
        back[b] = (g_hi, g_lo)

        @pl.when(has_hi)
        def _():
            g_hi.start()

        @pl.when(has_lo)
        def _():
            g_lo.start()

        act[b] = gelu_value(value).astype(BF16)

    def point_grad(j):
        return sum(dot_tn(cot[j, b], act[b]) for b in range(batch))

    if scatter:
        qs[0] = point_grad(s1).astype(BF16)
        qs[1] = point_grad(s3).astype(BF16)
        q1 = push(qs, qr, {"seq": s1})

    first = [None] * batch
    cross = [None] * batch
    for b in range(batch):
        g_hi, g_lo = back[b]

        @pl.when(has_hi)
        def _():
            g_lo.wait_recv()

        @pl.when(has_lo)
        def _():
            g_hi.wait_recv()

        for k in (3, 1, 2, 0):
            w_rows = chan_rows(peers[k])
            part[...] = dot_nt(dg[b], w_ref[1, w_rows, :])

            @pl.when(has_hi)
            def _():
                part[...] += dot_nt(dr_hi[b], w_ref[0, w_rows, :])

            @pl.when(has_lo)
            def _():
                part[...] += dot_nt(dr_lo[b], w_ref[2, w_rows, :])

            if k == 3:
                ps[b, 1] = part[...].astype(BF16)
                cross[b] = push(ps.at[b, 1], pr.at[b, 1], {"chan": c1})
            elif k == 1:
                ps[b, 0] = part[...].astype(BF16)
                first[b] = push(ps.at[b, 0], pr.at[b, 0], {"chan": c1})
            elif k == 2:
                cross[b].wait_recv()
                xs[b] = (part[...] + pr[b, 1].astype(F32)).astype(BF16)
                cross[b] = push(xs.at[b], xr.at[b], {"chan": c2})
            else:
                sg[b] = part[...]

    if scatter:
        q1.wait_recv()
        qs2[...] = (point_grad(s2) + qr[1].astype(F32)).astype(BF16)
        q2 = push(qs2, qr2, {"seq": s2})
        pg_ref[...] = point_grad(s) + qr[0].astype(F32)
    else:
        for j in range(4):
            pg_ref[j * width : (j + 1) * width, :] = point_grad(j)

    inner = [None] * batch
    for b in range(batch):
        first[b].wait_recv()
        cross[b].wait_recv()
        for at in range(0, rows, 128):
            here = slice(at, at + 128)
            raw = sg[b, here, :] + pr[b, 0, here, :].astype(F32) + xr[b, here, :].astype(F32)
            scaled = raw * slope[b, here, :]
            sg[b, here, :] = scaled
            unit = x_ref[b, here, :].astype(F32) * widen(rs[b, here, :], width)
            pn[b, 0, :, here] = jnp.broadcast_to(lanes_to_row(scaled * unit), (8, 128))
        inner[b] = [push(pn.at[b, 0], pn.at[b, k], {"chan": peers[k]}) for k in (2, 3, 1)]
    if scatter:
        q2.wait_recv()
        pg_ref[...] += qr2[...].astype(F32)
    for b in range(batch):
        for handle in inner[b]:
            handle.wait_recv()
        for at in range(0, rows, 128):
            here = slice(at, at + 128)
            total = pn[b, 0, 0:1, here] + pn[b, 1, 0:1, here] + pn[b, 2, 0:1, here] + pn[b, 3, 0:1, here]
            mean = widen(row_to_columns(total * (1.0 / channels)), width)
            scale = widen(rs[b, here, :], width)
            unit = x_ref[b, here, :].astype(F32) * scale
            out_ref[b, here, :] = (
                ct_ref[b, here, :].astype(F32) + scale * (sg[b, here, :] - unit * mean)
            ).astype(BF16)

    for handle in sent:
        handle.wait_send()
    for b in range(batch):
        for hi, lo in (halo[b], back[b]):

            @pl.when(has_hi)
            def _():
                hi.wait_send()

            @pl.when(has_lo)
            def _():
                lo.wait_send()


def per_device(seq_n, inputs, cotangent, dilated_weight, w_point, norm_gain):
    batch, rows, width = inputs.shape
    channels = norm_gain.shape[0]
    units = w_point.shape[1]
    scatter = seq_n * width == channels
    wide = lambda *lead: pltpu.VMEM((*lead, rows, width), BF16)
    thin = lambda *lead: pltpu.VMEM((*lead, rows, units), BF16)
    thin32 = lambda *lead: pltpu.VMEM((*lead, rows, units), F32)
    pg_rows = width if scatter else channels
    block = lambda *lead: pltpu.VMEM((*lead, width, units), BF16)
    vmem = pl.BlockSpec(memory_space=pltpu.VMEM)
    input_grad, point_grad = pl.pallas_call(
        functools.partial(kernel, seq_n, DILATION_STEP // rows, scatter),
        out_shape=(
            jax.ShapeDtypeStruct(inputs.shape, BF16),
            jax.ShapeDtypeStruct((pg_rows, units), F32),
        ),
        in_specs=[vmem] * 5,
        out_specs=(vmem, vmem),
        scratch_shapes=[
            wide(4, batch),
            wide(4, batch),
            pltpu.VMEM((4, 8, batch * rows), F32),
            pltpu.VMEM((batch, rows, 128), F32),
            pltpu.VMEM((batch, rows, width), F32),
            thin32(batch),
            thin32(),
            thin32(),
            thin(batch),
            thin32(batch),
            thin(batch), thin(batch), thin(batch), thin(batch),
            thin(batch), thin(batch), thin(batch),
            pltpu.VMEM((rows, width), F32),
            wide(batch, 2), wide(batch, 2),
            wide(batch), wide(batch),
            pltpu.VMEM((batch, rows, width), F32),
            pltpu.VMEM((batch, 4, 8, rows), F32),
            block(2), block(2), block(), block(),
            pltpu.SemaphoreType.DMA((N_SEMS,)),
            pltpu.SemaphoreType.DMA((N_SEMS,)),
        ],
        compiler_params=pltpu.CompilerParams(
            collective_id=0, has_side_effects=True, vmem_limit_bytes=40 * 1024 * 1024
        ),
    )(inputs, cotangent, dilated_weight, w_point, norm_gain.reshape(1, channels))
    if not scatter:
        point_grad = lax.psum_scatter(point_grad, "seq", scatter_dimension=0, tiled=True)
    return (input_grad, point_grad)


def solution(mesh):
    placed = (
        P("grp", "seq", "chan"),
        P("grp", "seq", "chan"),
        P(None, None, "chan"),
        P(None, "chan"),
        P(),
    )
    return jax.shard_map(
        functools.partial(per_device, mesh.shape["seq"]),
        mesh=mesh,
        in_specs=placed,
        out_specs=(P("grp", "seq", "chan"), P(("grp", "seq"), "chan")),
        check_vma=False,
    )
```

time: 199 us -> 71.1 us (0.36)
  waiting for transfers between devices: 148 us -> 0 us
  Pallas kernels: 0 us -> 59.1 us
  between operations: 14 us -> 0.68 us
  starting transfers between devices: 9.85 us -> 0 us
  matrix products: 8.55 us -> 0 us
  blocking collectives: 5.76 us -> 0 us
  other arithmetic: 4.65 us -> 0 us
  local copies, waits for them, and re-layouts: 8.36 us -> 10.9 us
    ppermute x4 -> x0, waiting for transfers between devices: 71.8 us -> none  [passed_along(): return lax.ppermute(block, axis, route)]
    pallas_call x0 -> x1, Pallas kernels: none -> 59.1 us  [per_device(): pl.pallas_call(functools.partial(kernel, seq_n, DILATION_STEP // rows, sc...]
    unnamed x5 -> x0, waiting for transfers between devices: 29.8 us -> none
    all_gather x2 -> x0, waiting for transfers between devices: 23.3 us -> none  [the longest x1 23.2 us: per_device(): lax.all_gather(inputs, 'chan', axis=2, tiled=True)]
    reduce_scatter x1 -> x0, waiting for transfers between devices: 22.8 us -> none  [per_device(): lax.psum_scatter(lax.dot_general(flat_grad, flat_active, (((0,), (0,)), (...]
    ppermute x4 -> x0, starting transfers between devices: 9.69 us -> none  [passed_along(): return lax.ppermute(block, axis, route)]
    dot_general x8 -> x0, matrix products: 8.55 us -> none  [the longest x4 4.08 us: forward_tap_rows(): jnp.einsum('bpc,ch->bph', values, weights, preferred_element_type=jnp.flo...]
    psum x1 -> x0, blocking collectives: 5.76 us -> none  [per_device(): lax.psum(jnp.sum(scaled_grad * unit, axis=-1, keepdims=True), 'chan')]
  transfers between devices with their start and end apart: 8 -> 0, of which waited for: 6 -> 0; matrix products, arithmetic and copies ran while one was open for 6% -> 0% of each run, Pallas kernels for 0% -> 0%
where the time goes in v2:
time: 71.1 us; the launch traced here: 70.7 us
  Pallas kernels  59.1 us (83%)
  local copies, waits for them, and re-layouts  10.9 us (15%)
    pallas_call x1, Pallas kernels, per_device(): pl.pallas_call(functools.partial(kernel, seq_n, DILATION_STEP // rows, sc...  59.1 us
    unnamed x11, local copies, waits for them, and re-layouts  8.34 us
    pallas_call x1, local copies, waits for them, and re-layouts, per_device(): pl.pallas_call(functools.partial(kernel, seq_n, DILATION_STEP // rows, sc...  1.86 us

profile of v2, /device:TPU:0, one launch (start us, length us, event | category | flops | bytes accessed | tf_op | source)
XLA Modules:
  0.0 70.7 jit_solution(11525077261504045789)
XLA Ops:
  0.6 0.7 reshape.7.gain_ref
  1.3 1.3 %copy.8.wp_ref = bf16[1536,192]{1,0:T(8,128)(2,1)S(1)} copy(bf16[1536,192]{0,1:T(8,128)(2,1)} %param.8) | data formatting | bytes 1179648 | tf_op args[3]
  2.7 0.0 copy-start
  2.7 2.7 %copy.7.w_ref = bf16[3,1536,192]{2,1,0:T(8,128)(2,1)S(1)} copy(bf16[3,1536,192]{1,2,0:T(8,128)(2,1)} %param.7) | data formatting | bytes 3538944 | tf_op args[2]
  5.4 0.0 copy-done
  5.4 0.0 copy-start.1
  5.5 1.0 %copy-done.1 = bf16[2,256,384]{2,1,0:T(8,128)(2,1)S(1)} copy-done((bf16[2,256,384]{2,1,0:T(8,128)(2,1)S(1)}, bf16[2,256,384]{2,1,0:T(8,128)(2,1)}, u32[]{:S(2)}) %copy-start.1) | copy-done | bytes 393240
  6.4 59.1 %shard_map.68 = (bf16[2,256,384]{2,1,0:T(8,128)(2,1)S(1)}, f32[384,192]{1,0:T(8,128)S(1)}) custom-call(bf16[2,256,384]{2,1,0:T(8,128)(2,1)S(1)} %copy-done, bf16[2,256,384]{2,1,0:T(8,128)(2,1)S(1)} %copy-done.1, bf16[3,1536,192]{2,1,0:T(8,128)(2,1)S(1)} %copy.7.w_ref, bf16[1536,192]{1,0:T(8,128)(2,1)S(1)} %copy.8.wp_ref, f32[1,1536]{1,0:T(1,128)S(1)} %reshape.7.gain_ref), custom_call_target="tpu_custom_call" | custom-call | tf_op jit(solution)/shard_map/pallas_call | solution.py:344
  65.5 0.0 copy-start.2
  65.5 0.7 %copy-done.2 = bf16[2,256,384]{2,1,0:T(8,128)(2,1)} copy-done((bf16[2,256,384]{2,1,0:T(8,128)(2,1)}, bf16[2,256,384]{2,1,0:T(8,128)(2,1)S(1)}, u32[]{:S(2)}) %copy-start.2) | copy-done | bytes 393240
  66.3 0.0 copy-start.3
  66.3 0.7 %copy-done.3 = f32[384,192]{1,0:T(8,128)} copy-done((f32[384,192]{1,0:T(8,128)}, f32[384,192]{1,0:T(8,128)S(1)}, u32[]{:S(2)}) %copy-start.3) | copy-done | bytes 294936
  67.0 1.9 %copy.9 = f32[384,192]{0,1:T(8,128)} copy(f32[384,192]{1,0:T(8,128)} %copy-done.3) | data formatting | bytes 589824 | tf_op jit(solution)/shard_map/pallas_call | solution.py:344
  68.9 1.8 %copy.11 = bf16[2,256,384]{2,1,0:T(8,128)(2,1)} copy(bf16[2,256,384]{2,1,0:T(8,128)(2,1)} %copy-done.2) | data formatting | bytes 786432
Async XLA Ops:
  2.7 2.8 %copy-start = (bf16[2,256,384]{2,1,0:T(8,128)(2,1)S(1)}, bf16[2,256,384]{2,1,0:T(8,128)(2,1)}, u32[]{:S(2)}) copy-start(bf16[2,256,384]{2,1,0:T(8,128)(2,1)} %x_ref.1) | copy-start | bytes 1179652
  5.4 1.0 %copy-start.1 = (bf16[2,256,384]{2,1,0:T(8,128)(2,1)S(1)}, bf16[2,256,384]{2,1,0:T(8,128)(2,1)}, u32[]{:S(2)}) copy-start(bf16[2,256,384]{2,1,0:T(8,128)(2,1)} %ct_ref.1) | copy-start | bytes 1179652
  65.5 0.7 %copy-start.2 = (bf16[2,256,384]{2,1,0:T(8,128)(2,1)}, bf16[2,256,384]{2,1,0:T(8,128)(2,1)S(1)}, u32[]{:S(2)}) copy-start(bf16[2,256,384]{2,1,0:T(8,128)(2,1)S(1)} %get-tuple-element.6) | copy-start | bytes 1179652
  66.3 0.7 %copy-start.3 = (f32[384,192]{1,0:T(8,128)}, f32[384,192]{1,0:T(8,128)S(1)}, u32[]{:S(2)}) copy-start(f32[384,192]{1,0:T(8,128)S(1)} %get-tuple-element.3) | copy-start | bytes 884740

commit v3 on v2

--- a/solution.py
+++ b/solution.py
@@ -54,9 +54,10 @@
 
 
 def kernel(
-    seq_n, stride, scatter, x_ref, ct_ref, w_ref, wp_ref, gain_ref, out_ref, pg_ref,
+    seq_n, stride, scatter, x_hbm, ct_hbm, w_hbm, wp_hbm, gain_ref, out_ref, pg_ref, qr2,
+    x_ref, w_ref, wp_ref,
     hid, cot, ss, rs, slope, dil, acc_lo, acc_hi, act, hg, y_lo, y_hi, yr_lo, yr_hi, dg, dr_lo, dr_hi,
-    part, ps, pr, xs, xr, sg, pn, qs, qr, qs2, qr2, send_sem, recv_sem,
+    part, ps, pr, xf, xs, xr, sg, pn, qs, qr, qs2, send_sem, recv_sem, load_sem,
 ):
     batch, rows, width = x_ref.shape
     channels = gain_ref.shape[1]
@@ -94,6 +95,15 @@
     def chan_rows(ch):
         return pl.ds(pl.multiple_of(ch * width, width), width)
 
+    loads = [
+        pltpu.make_async_copy(src, dst, load_sem.at[i])
+        for i, (src, dst) in enumerate(
+            ((x_hbm, x_ref), (ct_hbm, cot.at[c]), (w_hbm, w_ref), (wp_hbm, wp_ref))
+        )
+    ]
+    for load in loads:
+        load.start()
+
     barrier = pltpu.get_barrier_semaphore()
     for peer in (c1, c2, c3):
         pl.semaphore_signal(barrier, inc=1, device_id={"chan": peer}, device_id_type=MESH)
@@ -109,12 +119,13 @@
     if scatter:
         pl.semaphore_signal(barrier, inc=1, device_id={"seq": s1}, device_id_type=MESH)
 
+    loads[0].wait()
     for b in range(batch):
         for at in range(0, rows, 128):
             v = x_ref[b, at : at + 128, :].astype(F32)
             ss[0, :, b * rows + at : b * rows + at + 128] = jnp.broadcast_to(lanes_to_row(v * v), (8, 128))
 
-    cot[c] = ct_ref[...]
+    loads[1].wait()
     ways = has_hi.astype(jnp.int32) + has_lo.astype(jnp.int32)
     pl.semaphore_wait(barrier, ways + (4 if scatter else 3))
 
@@ -156,6 +167,8 @@
     normed_slope(0)
     relay_cot(0)
 
+    loads[2].wait()
+    loads[3].wait()
     halo = [None] * batch
     for b in range(batch):
         for k in range(4):
@@ -167,12 +180,12 @@
 
             @pl.when(has_hi)
             def _():
-                term = dot_nn(hid[k, b], w_ref[0, w_rows, :])
+                term = dot_nt(w_ref[0, :, w_rows], hid[k, b])
                 acc_hi[...] = term if k == 0 else acc_hi[...] + term
 
             @pl.when(has_lo)
             def _():
-                term = dot_nn(hid[k, b], w_ref[2, w_rows, :])
+                term = dot_nt(w_ref[2, :, w_rows], hid[k, b])
                 acc_lo[...] = term if k == 0 else acc_lo[...] + term
 
         to_hi = copy(y_hi.at[b], yr_lo.at[b], {"seq": up})
@@ -189,12 +202,12 @@
             y_lo[b] = acc_lo[...].astype(BF16)
             to_lo.start()
 
-        dil[b] = sum(dot_nn(hid[k, b], w_ref[1, chan_rows(peers[k]), :]) for k in range(4))
+        dil[b] = sum(dot_nt(w_ref[1, :, chan_rows(peers[k])], hid[k, b]) for k in range(4))
 
     def hidden_grad(b):
         cot_in[1][b].wait_recv()
         cot_in[3][b].wait_recv()
-        hg[b] = sum(dot_nn(cot[j, b], wp_ref[j * width : (j + 1) * width, :]) for j in range(4))
+        hg[b] = sum(dot_nt(wp_ref[:, j * width : (j + 1) * width], cot[j, b]) for j in range(4))
 
     hidden_grad(0)
     for b in range(1, batch):
@@ -234,59 +247,64 @@
         act[b] = gelu_value(value).astype(BF16)
 
     def point_grad(j):
-        return sum(dot_tn(cot[j, b], act[b]) for b in range(batch))
-
+        return sum(dot_nn(act[b], cot[j, b]) for b in range(batch))
+
+    first = [None] * batch
+    cross = [None] * batch
+
+    def partial_grads(b):
+        g_hi, g_lo = back[b]
+
+        @pl.when(has_hi)
+        def _():
+            g_lo.wait_recv()
+
+        @pl.when(has_lo)
+        def _():
+            g_hi.wait_recv()
+
+        part[...] = dot_tn(dg[b], w_ref[1])
+
+        @pl.when(has_hi)
+        def _():
+            part[...] += dot_tn(dr_hi[b], w_ref[0])
+
+        @pl.when(has_lo)
+        def _():
+            part[...] += dot_tn(dr_lo[b], w_ref[2])
+
+        ps[b, 1] = part[:, chan_rows(c3)].astype(BF16)
+        cross[b] = push(ps.at[b, 1], pr.at[b, 1], {"chan": c1})
+        ps[b, 0] = part[:, chan_rows(c1)].astype(BF16)
+        first[b] = push(ps.at[b, 0], pr.at[b, 0], {"chan": c1})
+        sg[b] = part[:, chan_rows(c)]
+        xf[b] = part[:, chan_rows(c2)]
+
+    def cross_over(b):
+        cross[b].wait_recv()
+        xs[b] = (xf[b] + pr[b, 1].astype(F32)).astype(BF16)
+        cross[b] = push(xs.at[b], xr.at[b], {"chan": c2})
+
+    partial_grads(0)
     if scatter:
         qs[0] = point_grad(s1).astype(BF16)
         qs[1] = point_grad(s3).astype(BF16)
         q1 = push(qs, qr, {"seq": s1})
-
-    first = [None] * batch
-    cross = [None] * batch
-    for b in range(batch):
-        g_hi, g_lo = back[b]
-
-        @pl.when(has_hi)
-        def _():
-            g_lo.wait_recv()
-
-        @pl.when(has_lo)
-        def _():
-            g_hi.wait_recv()
-
-        for k in (3, 1, 2, 0):
-            w_rows = chan_rows(peers[k])
-            part[...] = dot_nt(dg[b], w_ref[1, w_rows, :])
-
-            @pl.when(has_hi)
-            def _():
-                part[...] += dot_nt(dr_hi[b], w_ref[0, w_rows, :])
-
-            @pl.when(has_lo)
-            def _():
-                part[...] += dot_nt(dr_lo[b], w_ref[2, w_rows, :])
-
-            if k == 3:
-                ps[b, 1] = part[...].astype(BF16)
-                cross[b] = push(ps.at[b, 1], pr.at[b, 1], {"chan": c1})
-            elif k == 1:
-                ps[b, 0] = part[...].astype(BF16)
-                first[b] = push(ps.at[b, 0], pr.at[b, 0], {"chan": c1})
-            elif k == 2:
-                cross[b].wait_recv()
-                xs[b] = (part[...] + pr[b, 1].astype(F32)).astype(BF16)
-                cross[b] = push(xs.at[b], xr.at[b], {"chan": c2})
-            else:
-                sg[b] = part[...]
-
+    cross_over(0)
+    for b in range(1, batch):
+        partial_grads(b)
+        if scatter and b == 1:
+            pg_ref[...] = point_grad(s)
+        cross_over(b)
     if scatter:
         q1.wait_recv()
         qs2[...] = (point_grad(s2) + qr[1].astype(F32)).astype(BF16)
         q2 = push(qs2, qr2, {"seq": s2})
-        pg_ref[...] = point_grad(s) + qr[0].astype(F32)
+        pg_ref[...] += qr[0].astype(F32)
     else:
         for j in range(4):
-            pg_ref[j * width : (j + 1) * width, :] = point_grad(j)
+            pg_ref[:, j * width : (j + 1) * width] = point_grad(j)
+        qr2[...] = jnp.zeros(qr2.shape, BF16)
 
     inner = [None] * batch
     for b in range(batch):
@@ -302,7 +320,6 @@
         inner[b] = [push(pn.at[b, 0], pn.at[b, k], {"chan": peers[k]}) for k in (2, 3, 1)]
     if scatter:
         q2.wait_recv()
-        pg_ref[...] += qr2[...].astype(F32)
     for b in range(batch):
         for handle in inner[b]:
             handle.wait_recv()
@@ -312,9 +329,7 @@
             mean = widen(row_to_columns(total * (1.0 / channels)), width)
             scale = widen(rs[b, here, :], width)
             unit = x_ref[b, here, :].astype(F32) * scale
-            out_ref[b, here, :] = (
-                ct_ref[b, here, :].astype(F32) + scale * (sg[b, here, :] - unit * mean)
-            ).astype(BF16)
+            out_ref[b, here, :] = scale * (sg[b, here, :] - unit * mean)
 
     for handle in sent:
         handle.wait_send()
@@ -336,20 +351,25 @@
     units = w_point.shape[1]
     scatter = seq_n * width == channels
     wide = lambda *lead: pltpu.VMEM((*lead, rows, width), BF16)
-    thin = lambda *lead: pltpu.VMEM((*lead, rows, units), BF16)
-    thin32 = lambda *lead: pltpu.VMEM((*lead, rows, units), F32)
+    thin = lambda *lead: pltpu.VMEM((*lead, units, rows), BF16)
+    thin32 = lambda *lead: pltpu.VMEM((*lead, units, rows), F32)
     pg_rows = width if scatter else channels
-    block = lambda *lead: pltpu.VMEM((*lead, width, units), BF16)
+    block = lambda *lead: pltpu.VMEM((*lead, units, width), BF16)
     vmem = pl.BlockSpec(memory_space=pltpu.VMEM)
-    input_grad, point_grad = pl.pallas_call(
+    hbm = pl.BlockSpec(memory_space=pltpu.HBM)
+    branch_grad, point_grad, point_rest = pl.pallas_call(
         functools.partial(kernel, seq_n, DILATION_STEP // rows, scatter),
         out_shape=(
-            jax.ShapeDtypeStruct(inputs.shape, BF16),
-            jax.ShapeDtypeStruct((pg_rows, units), F32),
+            jax.ShapeDtypeStruct(inputs.shape, F32),
+            jax.ShapeDtypeStruct((units, pg_rows), F32),
+            jax.ShapeDtypeStruct((units, width), BF16),
         ),
-        in_specs=[vmem] * 5,
-        out_specs=(vmem, vmem),
+        in_specs=[hbm] * 4 + [vmem],
+        out_specs=(vmem, vmem, vmem),
         scratch_shapes=[
+            wide(batch),
+            pltpu.VMEM((3, units, channels), BF16),
+            pltpu.VMEM((units, channels), BF16),
             wide(4, batch),
             wide(4, batch),
             pltpu.VMEM((4, 8, batch * rows), F32),
@@ -362,20 +382,28 @@
             thin32(batch),
             thin(batch), thin(batch), thin(batch), thin(batch),
             thin(batch), thin(batch), thin(batch),
-            pltpu.VMEM((rows, width), F32),
+            pltpu.VMEM((rows, channels), F32),
             wide(batch, 2), wide(batch, 2),
+            pltpu.VMEM((batch, rows, width), F32),
             wide(batch), wide(batch),
             pltpu.VMEM((batch, rows, width), F32),
             pltpu.VMEM((batch, 4, 8, rows), F32),
-            block(2), block(2), block(), block(),
+            block(2), block(2), block(),
             pltpu.SemaphoreType.DMA((N_SEMS,)),
             pltpu.SemaphoreType.DMA((N_SEMS,)),
+            pltpu.SemaphoreType.DMA((4,)),
         ],
         compiler_params=pltpu.CompilerParams(
-            collective_id=0, has_side_effects=True, vmem_limit_bytes=40 * 1024 * 1024
+            collective_id=0, has_side_effects=True, vmem_limit_bytes=61 * 1024 * 1024
         ),
-    )(inputs, cotangent, dilated_weight, w_point, norm_gain.reshape(1, channels))
-    if not scatter:
+    )(
+        inputs, cotangent, dilated_weight.transpose(0, 2, 1), w_point.T, norm_gain.reshape(1, channels)
+    )
+    input_grad = (cotangent.astype(F32) + branch_grad).astype(BF16)
+    if scatter:
+        point_grad = (point_grad + point_rest.astype(F32)).T
+    else:
+        point_grad = point_grad.T
         point_grad = lax.psum_scatter(point_grad, "seq", scatter_dimension=0, tiled=True)
     return (input_grad, point_grad)
 

time: 71.1 us -> 59.7 us (0.84)
  local copies, waits for them, and re-layouts: 10.9 us -> 1.3 us
  Pallas kernels: 59.1 us -> 53.9 us
  other arithmetic: 0 us -> 3.69 us
    unnamed x11 -> x2, local copies, waits for them, and re-layouts: 8.34 us -> 0.01 us
    pallas_call x1, Pallas kernels: 59.1 us -> 53.9 us  [per_device(): pl.pallas_call(functools.partial(kernel, seq_n, DILATION_STEP // rows, sc...]
    convert_element_type x0 -> x1, other arithmetic: none -> 1.95 us  [per_device(): input_grad = (cotangent.astype(F32) + branch_grad).astype(BF16)]
    pallas_call x1 -> x0, local copies, waits for them, and re-layouts: 1.86 us -> none  [per_device(): pl.pallas_call(functools.partial(kernel, seq_n, DILATION_STEP // rows, sc...]
    transpose x0 -> x1, other arithmetic: none -> 1.74 us  [per_device(): point_grad = (point_grad + point_rest.astype(F32)).T]
where the time goes in v3:
time: 59.7 us; the launch traced here: 59.5 us
  Pallas kernels  53.9 us (90%)
  other arithmetic  3.69 us (6%)
  local copies, waits for them, and re-layouts  1.3 us (2%)
  between operations  0.64 us (1%)
    pallas_call x1, Pallas kernels, per_device(): pl.pallas_call(functools.partial(kernel, seq_n, DILATION_STEP // rows, sc...  53.9 us
    convert_element_type x1, other arithmetic, per_device(): input_grad = (cotangent.astype(F32) + branch_grad).astype(BF16)  1.95 us
    transpose x1, other arithmetic, per_device(): point_grad = (point_grad + point_rest.astype(F32)).T  1.74 us
    reshape x1, local copies, waits for them, and re-layouts, per_device(): norm_gain.reshape(1, channels)  1.29 us

profile of v3, /device:TPU:0, one launch (start us, length us, event | category | flops | bytes accessed | tf_op | source)
XLA Modules:
  0.0 59.5 jit_solution(1666032839253925150)
XLA Ops:
  0.6 1.3 %reshape.7.gain_ref = f32[1,1536]{1,0:T(1,128)} reshape(f32[1536]{0:T(1024)} %param.9) | data formatting | bytes 12288 | tf_op jit(solution)/shard_map/reshape | solution.py:400
  1.9 0.0 copy-start
  1.9 53.9 %shard_map.68 = (f32[2,256,384]{2,1,0:T(8,128)}, f32[192,384]{1,0:T(8,128)}, bf16[192,384]{1,0:T(8,128)(2,1)}) custom-call(bf16[2,256,384]{2,1,0:T(8,128)(2,1)} %x_hbm.1, bf16[2,256,384]{2,1,0:T(8,128)(2,1)} %ct_hbm.1, bf16[3,192,1536]{2,1,0:T(8,128)(2,1)} %bitcast.4, bf16[192,1536]{1,0:T(8,128)(2,1)} %bitcast.5, f32[1,1536]{1,0:T(1,128)} %reshape.7.gain_ref), custom_call_target="tpu_custom_call" | custom-call | tf_op jit(solution)/shard_map/pallas_call | solution.py:360
  55.8 1.7 %add_bitcast_fusion = f32[384,192]{0,1:T(8,128)} fusion(f32[192,384]{1,0:T(8,128)} %get-tuple-element.6, bf16[192,384]{1,0:T(8,128)(2,1)} %get-tuple-element.7), kind=kLoop, calls=%fused_computation.1 | loop fusion | flops 147456 | bytes 737280 | tf_op jit(solution)/shard_map/transpose | solution.py:404
  57.5 0.0 copy-done
  57.5 2.0 %add_convert_fusion = bf16[2,256,384]{2,1,0:T(8,128)(2,1)} fusion(f32[2,256,384]{2,1,0:T(8,128)} %get-tuple-element.5, bf16[2,256,384]{2,1,0:T(8,128)(2,1)S(1)} %copy-done), kind=kLoop, calls=%fused_computation | loop fusion | flops 589824 | bytes 1572864 | tf_op jit(solution)/shard_map/convert_element_type | solution.py:402
Async XLA Ops:
  1.9 55.6 %copy-start = (bf16[2,256,384]{2,1,0:T(8,128)(2,1)S(1)}, bf16[2,256,384]{2,1,0:T(8,128)(2,1)}, u32[]{:S(2)}) copy-start(bf16[2,256,384]{2,1,0:T(8,128)(2,1)} %ct_hbm.1) | copy-start | bytes 1179652

commit v4 on v3

--- a/solution.py
+++ b/solution.py
@@ -10,7 +10,7 @@
 
 DILATION_STEP = 512
 epsilon = 1e-05
-N_SEMS = 64
+N_SEMS = 96
 F32 = jnp.float32
 BF16 = jnp.bfloat16
 MESH = pl.DeviceIdType.MESH
@@ -346,7 +346,10 @@
 
 
 def per_device(seq_n, inputs, cotangent, dilated_weight, w_point, norm_gain):
-    batch, rows, width = inputs.shape
+    stride = DILATION_STEP // inputs.shape[1]
+    rows, width = 128, inputs.shape[2]
+    batch = inputs.shape[0] * inputs.shape[1] // rows
+    cut = (batch, rows, width)
     channels = norm_gain.shape[0]
     units = w_point.shape[1]
     scatter = seq_n * width == channels
@@ -358,9 +361,9 @@
     vmem = pl.BlockSpec(memory_space=pltpu.VMEM)
     hbm = pl.BlockSpec(memory_space=pltpu.HBM)
     branch_grad, point_grad, point_rest = pl.pallas_call(
-        functools.partial(kernel, seq_n, DILATION_STEP // rows, scatter),
+        functools.partial(kernel, seq_n, stride, scatter),
         out_shape=(
-            jax.ShapeDtypeStruct(inputs.shape, F32),
+            jax.ShapeDtypeStruct(cut, F32),
             jax.ShapeDtypeStruct((units, pg_rows), F32),
             jax.ShapeDtypeStruct((units, width), BF16),
         ),
@@ -397,9 +400,9 @@
             collective_id=0, has_side_effects=True, vmem_limit_bytes=61 * 1024 * 1024
         ),
     )(
-        inputs, cotangent, dilated_weight.transpose(0, 2, 1), w_point.T, norm_gain.reshape(1, channels)
+        inputs.reshape(cut), cotangent.reshape(cut), dilated_weight.transpose(0, 2, 1), w_point.T, norm_gain.reshape(1, channels)
     )
-    input_grad = (cotangent.astype(F32) + branch_grad).astype(BF16)
+    input_grad = (cotangent.astype(F32) + branch_grad.reshape(cotangent.shape)).astype(BF16)
     if scatter:
         point_grad = (point_grad + point_rest.astype(F32)).T
     else:

time: 59.7 us -> 59 us (0.988)
  Pallas kernels: 53.9 us -> 53.1 us
    pallas_call x1, Pallas kernels: 53.9 us -> 53.1 us  [per_device(): pl.pallas_call(functools.partial(kernel, seq_n, stride, scatter), out_sha...]
where the time goes in v4:
time: 59 us; the launch traced here: 58.8 us
  Pallas kernels  53.1 us (90%)
  other arithmetic  3.69 us (6%)
  local copies, waits for them, and re-layouts  1.3 us (2%)
  between operations  0.64 us (1%)
    pallas_call x1, Pallas kernels, per_device(): pl.pallas_call(functools.partial(kernel, seq_n, stride, scatter), out_sha...  53.1 us
    convert_element_type x1, other arithmetic, per_device(): (cotangent.astype(F32) + branch_grad.reshape(cotangent.shape)).astype(BF16)  1.95 us
    transpose x1, other arithmetic, per_device(): point_grad = (point_grad + point_rest.astype(F32)).T  1.74 us
    reshape x1, local copies, waits for them, and re-layouts, per_device(): norm_gain.reshape(1, channels)  1.29 us

profile of v4, /device:TPU:0, one launch (start us, length us, event | category | flops | bytes accessed | tf_op | source)
XLA Modules:
  0.0 58.8 jit_solution(12473979398186876169)
XLA Ops:
  0.6 1.3 %reshape.18.gain_ref = f32[1,1536]{1,0:T(1,128)} reshape(f32[1536]{0:T(1024)} %param.9) | data formatting | bytes 12288 | tf_op jit(solution)/shard_map/reshape | solution.py:403
  1.9 0.0 copy-start
  1.9 53.1 %shard_map.68 = (f32[4,128,384]{2,1,0:T(8,128)}, f32[192,384]{1,0:T(8,128)}, bf16[192,384]{1,0:T(8,128)(2,1)}) custom-call(bf16[4,128,384]{2,1,0:T(8,128)(2,1)} %bitcast.15, bf16[4,128,384]{2,1,0:T(8,128)(2,1)} %bitcast.12, bf16[3,192,1536]{2,1,0:T(8,128)(2,1)} %bitcast.11, bf16[192,1536]{1,0:T(8,128)(2,1)} %bitcast.14, f32[1,1536]{1,0:T(1,128)} %reshape.18.gain_ref), custom_call_target="tpu_custom_call" | custom-call | tf_op jit(solution)/shard_map/pallas_call | solution.py:363
  55.1 1.7 %add_bitcast_fusion = f32[384,192]{0,1:T(8,128)} fusion(f32[192,384]{1,0:T(8,128)} %get-tuple-element.6, bf16[192,384]{1,0:T(8,128)(2,1)} %get-tuple-element.7), kind=kLoop, calls=%fused_computation.2 | loop fusion | flops 147456 | bytes 737280 | tf_op jit(solution)/shard_map/transpose | solution.py:407
  56.8 0.0 copy-done
  56.8 2.0 %fusion = bf16[2,256,384]{2,1,0:T(8,128)(2,1)} fusion(bf16[2,256,384]{2,1,0:T(8,128)(2,1)S(1)} %copy-done, f32[2,256,384]{2,1,0:T(8,128)} %bitcast.13), kind=kLoop, calls=%fused_computation.1 | loop fusion | flops 589824 | bytes 1572864 | tf_op jit(solution)/shard_map/convert_element_type | solution.py:405
Async XLA Ops:
  1.9 54.9 %copy-start = (bf16[2,256,384]{2,1,0:T(8,128)(2,1)S(1)}, bf16[2,256,384]{2,1,0:T(8,128)(2,1)}, u32[]{:S(2)}) copy-start(bf16[2,256,384]{2,1,0:T(8,128)(2,1)} %param.6) | copy-start | bytes 1179652

commit v5 on v4

--- a/solution.py
+++ b/solution.py
@@ -212,7 +212,8 @@
     hidden_grad(0)
     for b in range(1, batch):
         normed_slope(b)
-        relay_cot(b)
+    if batch > 1:
+        relay_cot(1)
 
     back = [None] * batch
     for b in range(batch):
@@ -244,6 +245,8 @@
         def _():
             g_lo.start()
 
+        if b + 2 < batch:
+            relay_cot(b + 2)
         act[b] = gelu_value(value).astype(BF16)
 
     def point_grad(j):
@@ -293,9 +296,12 @@
     cross_over(0)
     for b in range(1, batch):
         partial_grads(b)
-        if scatter and b == 1:
+        if scatter and b == batch - 1:
             pg_ref[...] = point_grad(s)
-        cross_over(b)
+        if b > 1:
+            cross_over(b - 1)
+    if batch > 1:
+        cross_over(batch - 1)
     if scatter:
         q1.wait_recv()
         qs2[...] = (point_grad(s2) + qr[1].astype(F32)).astype(BF16)

time: 59 us -> 55.5 us (0.941)
  the two profiles are of different devices: /device:TPU:0 before, /device:TPU:2 now
where the time goes in v5:
time: 55.5 us; the launch traced here: 55.2 us
  Pallas kernels  49.6 us (89%)
  other arithmetic  3.69 us (7%)
  local copies, waits for them, and re-layouts  1.3 us (2%)
  between operations  0.64 us (1%)
    pallas_call x1, Pallas kernels, per_device(): pl.pallas_call(functools.partial(kernel, seq_n, stride, scatter), out_sha...  49.6 us
    convert_element_type x1, other arithmetic, per_device(): (cotangent.astype(F32) + branch_grad.reshape(cotangent.shape)).astype(BF16)  1.95 us
    transpose x1, other arithmetic, per_device(): point_grad = (point_grad + point_rest.astype(F32)).T  1.74 us
    reshape x1, local copies, waits for them, and re-layouts, per_device(): norm_gain.reshape(1, channels)  1.29 us

profile of v5, /device:TPU:2, one launch (start us, length us, event | category | flops | bytes accessed | tf_op | source)
XLA Modules:
  0.0 55.2 jit_solution(4665095347572379811)
XLA Ops:
  0.6 1.3 %reshape.18.gain_ref = f32[1,1536]{1,0:T(1,128)} reshape(f32[1536]{0:T(1024)} %param.9) | data formatting | bytes 12288 | tf_op jit(solution)/shard_map/reshape | solution.py:409
  1.9 0.0 copy-start
  1.9 49.6 %shard_map.68 = (f32[4,128,384]{2,1,0:T(8,128)}, f32[192,384]{1,0:T(8,128)}, bf16[192,384]{1,0:T(8,128)(2,1)}) custom-call(bf16[4,128,384]{2,1,0:T(8,128)(2,1)} %bitcast.15, bf16[4,128,384]{2,1,0:T(8,128)(2,1)} %bitcast.12, bf16[3,192,1536]{2,1,0:T(8,128)(2,1)} %bitcast.11, bf16[192,1536]{1,0:T(8,128)(2,1)} %bitcast.14, f32[1,1536]{1,0:T(1,128)} %reshape.18.gain_ref), custom_call_target="tpu_custom_call" | custom-call | tf_op jit(solution)/shard_map/pallas_call | solution.py:369
  51.5 1.7 %add_bitcast_fusion = f32[384,192]{0,1:T(8,128)} fusion(f32[192,384]{1,0:T(8,128)} %get-tuple-element.6, bf16[192,384]{1,0:T(8,128)(2,1)} %get-tuple-element.7), kind=kLoop, calls=%fused_computation.2 | loop fusion | flops 147456 | bytes 737280 | tf_op jit(solution)/shard_map/transpose | solution.py:413
  53.3 0.0 copy-done
  53.3 2.0 %fusion = bf16[2,256,384]{2,1,0:T(8,128)(2,1)} fusion(bf16[2,256,384]{2,1,0:T(8,128)(2,1)S(1)} %copy-done, f32[2,256,384]{2,1,0:T(8,128)} %bitcast.13), kind=kLoop, calls=%fused_computation.1 | loop fusion | flops 589824 | bytes 1572864 | tf_op jit(solution)/shard_map/convert_element_type | solution.py:411
Async XLA Ops:
  1.9 51.4 %copy-start = (bf16[2,256,384]{2,1,0:T(8,128)(2,1)S(1)}, bf16[2,256,384]{2,1,0:T(8,128)(2,1)}, u32[]{:S(2)}) copy-start(bf16[2,256,384]{2,1,0:T(8,128)(2,1)} %param.6) | copy-start | bytes 1179652
